TPU v7x, 32 devices: a whole 2x2x4 slice. The times are simulated.
32 devices in a mesh: box: 8 (over y, x, core), group: 4 (over z).
Axes of the slice: x: 2, y: 2, z: 4, core: 2. Of those that a mesh axis runs over, the one named last changes fastest.
Arguments:
- right_side: float32 [128, 128, 512], P('box', 'group'), may hold values from -6 to 6
- inv_density: float32 [128, 128, 512], P('box', 'group'), may hold values from 0.2 to 5
- pressure: float32 [128, 128, 512], P('box', 'group'), may hold values from -6 to 6
Outputs:
- corrected: float32 [128, 128, 512], P('box', 'group')
All inputs are finite; a program needn't handle non-finite values.
Results may differ from a plain program's by a relative error of at most 0.0003.
Values sent between devices are 32-bit elements; how exact they have to be, the bound alone decides.
A program may use at most 128 MiB of HBM per device.

v0:
```python
import jax
import jax.numpy as jnp
from jax import lax
from jax.sharding import PartitionSpec as P

SWEEPS = 2
CHEB = 8


def extended(block, sides, width):
    for axis, dim in sides:
        count = lax.axis_size(axis)
        forward = [(i, i + 1) for i in range(count - 1)]
        backward = [(target, source) for source, target in forward]
        low = lax.ppermute(
            lax.slice_in_dim(block, block.shape[dim] - width, None, axis=dim), axis, forward
        )
        high = lax.ppermute(lax.slice_in_dim(block, 0, width, axis=dim), axis, backward)
        block = jnp.concatenate([low, block, high], axis=dim)
    return block


def neighbours(padded):
    return [
        padded[:-2, 1:-1, 1:-1],
        padded[2:, 1:-1, 1:-1],
        padded[1:-1, :-2, 1:-1],
        padded[1:-1, 2:, 1:-1],
        padded[1:-1, 1:-1, :-2],
        padded[1:-1, 1:-1, 2:],
    ]


def face_coefs(field, padded):
    return [
        jnp.where(near > 0, 2.0 * field * near / (field + near), field)
        for near in neighbours(padded)
    ]


def stencil(field, padded, coefs):
    total = jnp.zeros_like(field)
    for coef, near in zip(coefs, neighbours(padded)):
        total = total + coef * (field - near)
    return total


def block_mean(field):
    sx, sy, sz = field.shape
    return field.reshape(sx // 4, 4, sy // 4, 4, sz // 4, 4).mean(axis=(1, 3, 5))


def chebyshev(rhs_c, coefs, diag, padder):
    low, high = (0.05, 2.0)
    theta = (high + low) / 2.0
    delta = (high - low) / 2.0
    sigma = theta / delta
    rho = 1.0 / sigma
    solution = jnp.zeros_like(rhs_c)
    remain = rhs_c
    direction = remain / (diag * theta)
    for step in range(CHEB):
        solution = solution + direction
        if step + 1 < CHEB:
            remain = remain - stencil(direction, padder(direction), coefs)
            rho_next = 1.0 / (2.0 * sigma - rho)
            direction = rho_next * rho * direction + 2.0 * rho_next / delta * remain / diag
            rho = rho_next
    return solution


def depth_pad(field):
    return jnp.pad(field, ((0, 0), (0, 0), (1, 1)))


def sweep_pad(field):
    return depth_pad(extended(field, (("box", 0), ("group", 1)), 1))


def direction_pad(field):
    return depth_pad(extended(field, (("box", 0), ("group", 1)), 1))


def per_device(right_side, inv_density, pressure):
    stacked = jnp.stack([pressure, inv_density])
    padded = extended(stacked, (("box", 1), ("group", 2)), 1)
    coefs = face_coefs(inv_density, depth_pad(padded[1]))
    diag = sum(coefs)
    fine = pressure
    fine_padded = depth_pad(padded[0])
    for sweep in range(SWEEPS):
        fine = fine + 2.0 / 3.0 * (right_side - stencil(fine, fine_padded, coefs)) / diag
        fine_padded = sweep_pad(fine)
    res = right_side - stencil(fine, fine_padded, coefs)
    coarse_rhs = block_mean(res)
    coarse_b = block_mean(inv_density)
    coarse_padded = depth_pad(extended(coarse_b, (("box", 0), ("group", 1)), 1))
    coarse_coefs = [c * 0.0625 for c in face_coefs(coarse_b, coarse_padded)]
    corr = chebyshev(coarse_rhs, coarse_coefs, sum(coarse_coefs), direction_pad)
    expanded = jnp.repeat(jnp.repeat(jnp.repeat(corr, 4, axis=0), 4, axis=1), 4, axis=2)
    return fine + expanded


def solution(mesh):
    return jax.shard_map(
        per_device,
        mesh=mesh,
        in_specs=(P("box", "group", None), P("box", "group", None), P("box", "group", None)),
        out_specs=P("box", "group", None),
        check_vma=False,
    )
```

profile of v0, /device:TPU:5, one launch (start us, length us, event | category | flops | bytes accessed | tf_op | source)
XLA Modules:
  0.0 284.7 jit_solution(15951417977219399274)
XLA Ops:
  1.1 3.7 %collective-permute-start = (f32[2,1,32,512]{3,2,1,0:T(8,128)S(1)}, f32[2,1,32,512]{3,2,1,0:T(8,128)S(1)}, u32[]{:S(2)}, u32[]{:S(2)}) collective-permute-start(f32[2,1,32,512]{3,2,1,0:T(8,128)S(1)} %get-tuple-element.27), channel_id=1, source_target_pairs={{0,4},{4,8},{8,12},{12,16},{16,20},{20,24},{24,28},{1,5},{5,9},{9,... | collective-permute-start | bytes 393224 | tf_op jit(solution)/shard_map/ppermute | solution.py:15
  4.8 1.9 collective-permute-start.1
  6.7 4.3 %collective-permute-done.1 = f32[2,1,32,512]{3,2,1,0:T(8,128)S(1)} collective-permute-done((f32[2,1,32,512]{3,2,1,0:T(8,128)S(1)}, f32[2,1,32,512]{3,2,1,0:T(8,128)S(1)}, u32[]{:S(2)}, u32[]{:S(2)}) %collective-permute-start.1) | collective-permute-done | bytes 131104 | tf_op jit(solution)/shard_map/ppermute | solution.py:18
  11.3 1.3 collective-permute-start.3
  12.6 4.0 %collective-permute-start.2 = (f32[2,18,1,512]{3,0,2,1:T(2,128)S(1)}, f32[2,18,1,512]{3,0,2,1:T(2,128)S(1)}, u32[]{:S(2)}, u32[]{:S(2)}) collective-permute-start(f32[2,18,1,512]{3,0,2,1:T(2,128)S(1)} %copy.166), channel_id=1, source_target_pairs={{0,1},{1,2},{2,3},{4,5},{5,6},{6,7},{8,9},{9,10},{10,11},{12,13},{... | collective-permute-start | bytes 221192 | tf_op jit(solution)/shard_map/ppermute | solution.py:15
  16.6 35.9 %reshape.16 = f32[4,4,8,4,128,4]{5,4,3,2,1,0:T(8,128)} reshape(f32[16,32,512]{2,1,0:T(8,128)S(1)} %copy-done) | data formatting | bytes 2097152 | tf_op jit(solution)/shard_map/reshape | solution.py:50
  52.5 12.2 %reduce_sum.19 = f32[4,8,128]{2,1,0:T(8,128)S(1)} reduce(f32[4,4,8,4,128,4]{5,4,3,2,1,0:T(8,128)} %reshape.16, f32[]{:T(128)} %constant.21.clone.1), dimensions={1,3,5}, to_apply=%region_1.2 | reduce | flops 258048 | bytes 1064964 | tf_op jit(solution)/shard_map/reduce_sum | solution.py:50
  66.6 3.8 %fusion.8 = f32[16,32,512]{2,1,0:T(8,128)S(1)} fusion(f32[16,32,512]{2,1,0:T(8,128)S(1)} %copy-done.1, f32[16,32,512]{2,1,0:T(8,128)S(1)} %copy-done.2, f32[18,34,512]{2,1,0:T(8,128)S(1)} %get-tuple-element.24, f32[16,32,512]{2,1,0:T(8,128)S(1)} %copy-done, f32[18,34,512]{2,1,0:T(8,128)S(1)} %get-tuple-element.23), kind=kLoop, calls=%fused_computation.25 | loop fusion | flops 14942208 | bytes 15532032 | tf_op jit(solution)/shard_map/add | solution.py:92
  70.4 2.3 collective-permute-start.4
  72.8 2.0 collective-permute-start.5
  74.8 3.6 %collective-permute-done.5 = f32[1,32,512]{2,1,0:T(8,128)S(1)} collective-permute-done((f32[1,32,512]{2,1,0:T(8,128)S(1)}, f32[1,32,512]{2,1,0:T(8,128)S(1)}, u32[]{:S(2)}, u32[]{:S(2)}) %collective-permute-start.5) | collective-permute-done | bytes 65568 | tf_op jit(solution)/shard_map/ppermute | solution.py:18
  78.4 3.2 %collective-permute-start.6 = (f32[18,1,512]{2,1,0:T(1,128)S(1)}, f32[18,1,512]{2,1,0:T(1,128)S(1)}, u32[]{:S(2)}, u32[]{:S(2)}) collective-permute-start(f32[18,1,512]{2,1,0:T(1,128)S(1)} %get-tuple-element.31), channel_id=1, source_target_pairs={{0,1},{1,2},{2,3},{4,5},{5,6},{6,7},{8,9},{9,10},{10,11},{12,13},{... | collective-permute-start | bytes 110600 | tf_op jit(solution)/shard_map/ppermute | solution.py:15
  81.7 1.3 collective-permute-start.7
  83.0 2.1 collective-permute-start.12
  85.1 2.6 collective-permute-start.13
  88.6 4.9 %fusion.32 = f32[16,32,512]{2,1,0:T(8,128)S(1)} fusion(f32[16,32,512]{2,1,0:T(8,128)S(1)} %fusion.8, f32[16,32,512]{2,1,0:T(8,128)S(1)} %copy-done.2, f32[18,34,514]{2,1,0:T(8,128)S(1)} %select_maximum_fusion.4, f32[18,1,512]{2,1,0:T(1,128)S(1)} %collective-permute-done.7, f32[1,32,512]{2,1,0:T(8,128)S(1)} %collective-permute-done.5, ...), kind=kLoop, calls=%fused_computation.60 | loop fusion | flops 17039360 | bytes 12165120 | tf_op jit(solution)/shard_map/add | solution.py:92
  93.5 2.9 %collective-permute-start.8 = (f32[1,32,512]{2,1,0:T(8,128)S(1)}, f32[1,32,512]{2,1,0:T(8,128)S(1)}, u32[]{:S(2)}, u32[]{:S(2)}) collective-permute-start(f32[1,32,512]{2,1,0:T(8,128)S(1)} %get-tuple-element.33), channel_id=1, source_target_pairs={{0,4},{4,8},{8,12},{12,16},{16,20},{20,24},{24,28},{1,5},{5,9},{9,... | collective-permute-start | bytes 196616 | tf_op jit(solution)/shard_map/ppermute | solution.py:15
  96.5 3.5 %collective-permute-start.9 = (f32[1,32,512]{2,1,0:T(8,128)S(1)}, f32[1,32,512]{2,1,0:T(8,128)S(1)}, u32[]{:S(2)}, u32[]{:S(2)}) collective-permute-start(f32[1,32,512]{2,1,0:T(8,128)S(1)} %get-tuple-element.34), channel_id=1, source_target_pairs={{4,0},{8,4},{12,8},{16,12},{20,16},{24,20},{28,24},{5,1},{9,5},{13... | collective-permute-start | bytes 196616 | tf_op jit(solution)/shard_map/ppermute | solution.py:18
  100.1 1.3 collective-permute-start.15
  101.4 4.9 %collective-permute-start.14 = (f32[6,1,128]{2,1,0:T(1,128)S(1)}, f32[6,1,128]{2,1,0:T(1,128)S(1)}, u32[]{:S(2)}, u32[]{:S(2)}) collective-permute-start(f32[6,1,128]{2,1,0:T(1,128)S(1)} %get-tuple-element.52), channel_id=1, source_target_pairs={{0,1},{1,2},{2,3},{4,5},{5,6},{6,7},{8,9},{9,10},{10,11},{12,13},{... | collective-permute-start | bytes 9224 | tf_op jit(solution)/shard_map/ppermute | solution.py:15
  106.4 3.4 %collective-permute-start.10 = (f32[18,1,512]{2,1,0:T(1,128)S(1)}, f32[18,1,512]{2,1,0:T(1,128)S(1)}, u32[]{:S(2)}, u32[]{:S(2)}) collective-permute-start(f32[18,1,512]{2,1,0:T(1,128)S(1)} %get-tuple-element.29), channel_id=1, source_target_pairs={{0,1},{1,2},{2,3},{4,5},{5,6},{6,7},{8,9},{9,10},{10,11},{12,13},{... | collective-permute-start | bytes 110600 | tf_op jit(solution)/shard_map/ppermute | solution.py:15
  109.7 1.5 collective-permute-start.11
  111.4 3.1 %collective-permute-done.11 = f32[18,1,512]{2,1,0:T(1,128)S(1)} collective-permute-done((f32[18,1,512]{2,1,0:T(1,128)S(1)}, f32[18,1,512]{2,1,0:T(1,128)S(1)}, u32[]{:S(2)}, u32[]{:S(2)}) %collective-permute-start.11) | collective-permute-done | bytes 36896 | tf_op jit(solution)/shard_map/ppermute | solution.py:18
  115.3 4.6 %fusion.13 = f32[16,32,512]{2,1,0:T(8,128)S(1)} fusion(f32[16,32,512]{2,1,0:T(8,128)S(1)} %copy-done.2, f32[16,32,512]{2,1,0:T(8,128)S(1)} %fusion.32, f32[18,34,514]{2,1,0:T(8,128)S(1)} %select_maximum_fusion, f32[18,1,512]{2,1,0:T(1,128)S(1)} %collective-permute-done.11, f32[1,32,512]{2,1,0:T(8,128)S(1)} %collective-permute-done.9, ...), kind=kLoop, calls=%fused_computation.31 | loop fusion | flops 14942208 | bytes 12165120 | tf_op jit(solution)/shard_map/sub | solution.py:94
  119.9 35.9 %reshape.15 = f32[4,4,8,4,128,4]{5,4,3,2,1,0:T(8,128)} reshape(f32[16,32,512]{2,1,0:T(8,128)S(1)} %fusion.13) | data formatting | bytes 2097152 | tf_op jit(solution)/shard_map/reshape | solution.py:50
  155.8 12.2 %reduce_sum.18 = f32[4,8,128]{2,1,0:T(8,128)S(1)} reduce(f32[4,4,8,4,128,4]{5,4,3,2,1,0:T(8,128)} %reshape.15, f32[]{:T(128)} %constant.21.clone.1), dimensions={1,3,5}, to_apply=%region_0.1 | reduce | flops 258048 | bytes 1064964 | tf_op jit(solution)/shard_map/reduce_sum | solution.py:50
  168.1 4.0 %collective-permute-start.16 = (f32[1,8,128]{2,1,0:T(8,128)S(1)}, f32[1,8,128]{2,1,0:T(8,128)S(1)}, u32[]{:S(2)}, u32[]{:S(2)}) collective-permute-start(f32[1,8,128]{2,1,0:T(8,128)S(1)} %get-tuple-element.65), channel_id=1, source_target_pairs={{0,4},{4,8},{8,12},{12,16},{16,20},{20,24},{24,28},{1,5},{5,9},{9,... | collective-permute-start | bytes 12296 | tf_op jit(solution)/shard_map/ppermute | solution.py:15
  172.2 4.4 %collective-permute-start.17 = (f32[1,8,128]{2,1,0:T(8,128)S(1)}, f32[1,8,128]{2,1,0:T(8,128)S(1)}, u32[]{:S(2)}, u32[]{:S(2)}) collective-permute-start(f32[1,8,128]{2,1,0:T(8,128)S(1)} %get-tuple-element.66), channel_id=1, source_target_pairs={{4,0},{8,4},{12,8},{16,12},{20,16},{24,20},{28,24},{5,1},{9,5},{13... | collective-permute-start | bytes 12296 | tf_op jit(solution)/shard_map/ppermute | solution.py:18
  177.4 3.2 %collective-permute-start.18 = (f32[6,1,128]{2,1,0:T(1,128)S(1)}, f32[6,1,128]{2,1,0:T(1,128)S(1)}, u32[]{:S(2)}, u32[]{:S(2)}) collective-permute-start(f32[6,1,128]{2,1,0:T(1,128)S(1)} %get-tuple-element.49), channel_id=1, source_target_pairs={{0,1},{1,2},{2,3},{4,5},{5,6},{6,7},{8,9},{9,10},{10,11},{12,13},{... | collective-permute-start | bytes 9224 | tf_op jit(solution)/shard_map/ppermute | solution.py:15
  180.6 1.3 collective-permute-start.19
  181.9 3.0 %collective-permute-done.19 = f32[6,1,128]{2,1,0:T(1,128)S(1)} collective-permute-done((f32[6,1,128]{2,1,0:T(1,128)S(1)}, f32[6,1,128]{2,1,0:T(1,128)S(1)}, u32[]{:S(2)}, u32[]{:S(2)}) %collective-permute-start.19) | collective-permute-done | bytes 3104 | tf_op jit(solution)/shard_map/ppermute | solution.py:18
  185.2 3.1 %collective-permute-start.20 = (f32[1,8,128]{2,1,0:T(8,128)S(1)}, f32[1,8,128]{2,1,0:T(8,128)S(1)}, u32[]{:S(2)}, u32[]{:S(2)}) collective-permute-start(f32[1,8,128]{2,1,0:T(8,128)S(1)} %get-tuple-element.63), channel_id=1, source_target_pairs={{0,4},{4,8},{8,12},{12,16},{16,20},{20,24},{24,28},{1,5},{5,9},{9,... | collective-permute-start | bytes 12296 | tf_op jit(solution)/shard_map/ppermute | solution.py:15
  188.3 5.3 %collective-permute-start.21 = (f32[1,8,128]{2,1,0:T(8,128)S(1)}, f32[1,8,128]{2,1,0:T(8,128)S(1)}, u32[]{:S(2)}, u32[]{:S(2)}) collective-permute-start(f32[1,8,128]{2,1,0:T(8,128)S(1)} %get-tuple-element.64), channel_id=1, source_target_pairs={{4,0},{8,4},{12,8},{16,12},{20,16},{24,20},{28,24},{5,1},{9,5},{13... | collective-permute-start | bytes 12296 | tf_op jit(solution)/shard_map/ppermute | solution.py:18
  194.4 1.6 collective-permute-start.22
  196.0 1.3 collective-permute-start.23
  197.4 3.0 %collective-permute-done.23 = f32[6,1,128]{2,1,0:T(1,128)S(1)} collective-permute-done((f32[6,1,128]{2,1,0:T(1,128)S(1)}, f32[6,1,128]{2,1,0:T(1,128)S(1)}, u32[]{:S(2)}, u32[]{:S(2)}) %collective-permute-start.23) | collective-permute-done | bytes 3104 | tf_op jit(solution)/shard_map/ppermute | solution.py:18
  200.6 2.2 collective-permute-start.24
  202.8 6.2 %collective-permute-start.25 = (f32[1,8,128]{2,1,0:T(8,128)S(1)}, f32[1,8,128]{2,1,0:T(8,128)S(1)}, u32[]{:S(2)}, u32[]{:S(2)}) collective-permute-start(f32[1,8,128]{2,1,0:T(8,128)S(1)} %get-tuple-element.62), channel_id=1, source_target_pairs={{4,0},{8,4},{12,8},{16,12},{20,16},{24,20},{28,24},{5,1},{9,5},{13... | collective-permute-start | bytes 12296 | tf_op jit(solution)/shard_map/ppermute | solution.py:18
  209.8 1.6 collective-permute-start.26
  211.5 1.3 collective-permute-start.27
  212.8 3.0 %collective-permute-done.27 = f32[6,1,128]{2,1,0:T(1,128)S(1)} collective-permute-done((f32[6,1,128]{2,1,0:T(1,128)S(1)}, f32[6,1,128]{2,1,0:T(1,128)S(1)}, u32[]{:S(2)}, u32[]{:S(2)}) %collective-permute-start.27) | collective-permute-done | bytes 3104 | tf_op jit(solution)/shard_map/ppermute | solution.py:18
  216.0 1.9 collective-permute-start.28
  218.0 6.5 %collective-permute-start.29 = (f32[1,8,128]{2,1,0:T(8,128)S(1)}, f32[1,8,128]{2,1,0:T(8,128)S(1)}, u32[]{:S(2)}, u32[]{:S(2)}) collective-permute-start(f32[1,8,128]{2,1,0:T(8,128)S(1)} %get-tuple-element.60), channel_id=1, source_target_pairs={{4,0},{8,4},{12,8},{16,12},{20,16},{24,20},{28,24},{5,1},{9,5},{13... | collective-permute-start | bytes 12296 | tf_op jit(solution)/shard_map/ppermute | solution.py:18
  225.3 1.6 collective-permute-start.30
  226.9 1.3 collective-permute-start.31
  228.2 3.0 %collective-permute-done.31 = f32[6,1,128]{2,1,0:T(1,128)S(1)} collective-permute-done((f32[6,1,128]{2,1,0:T(1,128)S(1)}, f32[6,1,128]{2,1,0:T(1,128)S(1)}, u32[]{:S(2)}, u32[]{:S(2)}) %collective-permute-start.31) | collective-permute-done | bytes 3104 | tf_op jit(solution)/shard_map/ppermute | solution.py:18
  231.5 1.9 collective-permute-start.32
  233.4 6.5 %collective-permute-start.33 = (f32[1,8,128]{2,1,0:T(8,128)S(1)}, f32[1,8,128]{2,1,0:T(8,128)S(1)}, u32[]{:S(2)}, u32[]{:S(2)}) collective-permute-start(f32[1,8,128]{2,1,0:T(8,128)S(1)} %get-tuple-element.58), channel_id=1, source_target_pairs={{4,0},{8,4},{12,8},{16,12},{20,16},{24,20},{28,24},{5,1},{9,5},{13... | collective-permute-start | bytes 12296 | tf_op jit(solution)/shard_map/ppermute | solution.py:18
  240.7 1.6 collective-permute-start.34
  242.3 1.3 collective-permute-start.35
  243.6 3.0 %collective-permute-done.35 = f32[6,1,128]{2,1,0:T(1,128)S(1)} collective-permute-done((f32[6,1,128]{2,1,0:T(1,128)S(1)}, f32[6,1,128]{2,1,0:T(1,128)S(1)}, u32[]{:S(2)}, u32[]{:S(2)}) %collective-permute-start.35) | collective-permute-done | bytes 3104 | tf_op jit(solution)/shard_map/ppermute | solution.py:18
  246.9 1.9 collective-permute-start.36
  248.8 6.5 %collective-permute-start.37 = (f32[1,8,128]{2,1,0:T(8,128)S(1)}, f32[1,8,128]{2,1,0:T(8,128)S(1)}, u32[]{:S(2)}, u32[]{:S(2)}) collective-permute-start(f32[1,8,128]{2,1,0:T(8,128)S(1)} %get-tuple-element.56), channel_id=1, source_target_pairs={{4,0},{8,4},{12,8},{16,12},{20,16},{24,20},{28,24},{5,1},{9,5},{13... | collective-permute-start | bytes 12296 | tf_op jit(solution)/shard_map/ppermute | solution.py:18
  256.1 1.6 collective-permute-start.38
  257.8 1.3 collective-permute-start.39
  259.1 3.0 %collective-permute-done.39 = f32[6,1,128]{2,1,0:T(1,128)S(1)} collective-permute-done((f32[6,1,128]{2,1,0:T(1,128)S(1)}, f32[6,1,128]{2,1,0:T(1,128)S(1)}, u32[]{:S(2)}, u32[]{:S(2)}) %collective-permute-start.39) | collective-permute-done | bytes 3104 | tf_op jit(solution)/shard_map/ppermute | solution.py:18
  262.3 1.9 collective-permute-start.40
  264.3 6.5 %collective-permute-start.41 = (f32[1,8,128]{2,1,0:T(8,128)S(1)}, f32[1,8,128]{2,1,0:T(8,128)S(1)}, u32[]{:S(2)}, u32[]{:S(2)}) collective-permute-start(f32[1,8,128]{2,1,0:T(8,128)S(1)} %get-tuple-element.54), channel_id=1, source_target_pairs={{4,0},{8,4},{12,8},{16,12},{20,16},{24,20},{28,24},{5,1},{9,5},{13... | collective-permute-start | bytes 12296 | tf_op jit(solution)/shard_map/ppermute | solution.py:18
  271.6 1.6 collective-permute-start.42
  273.2 1.3 collective-permute-start.43
  274.5 3.0 %collective-permute-done.43 = f32[6,1,128]{2,1,0:T(1,128)S(1)} collective-permute-done((f32[6,1,128]{2,1,0:T(1,128)S(1)}, f32[6,1,128]{2,1,0:T(1,128)S(1)}, u32[]{:S(2)}, u32[]{:S(2)}) %collective-permute-start.43) | collective-permute-done | bytes 3104 | tf_op jit(solution)/shard_map/ppermute | solution.py:18
  278.4 2.3 broadcast_in_dim.11
  280.7 2.8 copy.165
  283.5 1.2 add.379
  (91 shorter events, 12.9 us)
Async XLA Ops:
  0.0 11.1 %copy-start = (f32[16,32,512]{2,1,0:T(8,128)S(1)}, f32[16,32,512]{2,1,0:T(8,128)}, u32[]{:S(2)}) copy-start(f32[16,32,512]{2,1,0:T(8,128)} %param.4) | copy-start | bytes 3145732
  0.0 11.1 %copy-start.1 = (f32[16,32,512]{2,1,0:T(8,128)S(1)}, f32[16,32,512]{2,1,0:T(8,128)}, u32[]{:S(2)}) copy-start(f32[16,32,512]{2,1,0:T(8,128)} %param.5) | copy-start | bytes 3145732
  1.1 5.6 %collective-permute-start = (f32[2,1,32,512]{3,2,1,0:T(8,128)S(1)}, f32[2,1,32,512]{3,2,1,0:T(8,128)S(1)}, u32[]{:S(2)}, u32[]{:S(2)}) collective-permute-start(f32[2,1,32,512]{3,2,1,0:T(8,128)S(1)} %get-tuple-element.27), channel_id=1, source_target_pairs={{0,4},{4,8},{8,12},{12,16},{16,20},{20,24},{24,28},{1,5},{5,9},{9,... | collective-permute-start | bytes 393224 | tf_op jit(solution)/shard_map/ppermute | solution.py:15
  4.8 6.3 %collective-permute-start.1 = (f32[2,1,32,512]{3,2,1,0:T(8,128)S(1)}, f32[2,1,32,512]{3,2,1,0:T(8,128)S(1)}, u32[]{:S(2)}, u32[]{:S(2)}) collective-permute-start(f32[2,1,32,512]{3,2,1,0:T(8,128)S(1)} %get-tuple-element.28), channel_id=1, source_target_pairs={{4,0},{8,4},{12,8},{16,12},{20,16},{24,20},{28,24},{5,1},{9,5},{13... | collective-permute-start | bytes 393224 | tf_op jit(solution)/shard_map/ppermute | solution.py:18
  11.3 53.5 %collective-permute-start.3 = (f32[2,18,1,512]{3,0,2,1:T(2,128)S(1)}, f32[2,18,1,512]{3,0,2,1:T(2,128)S(1)}, u32[]{:S(2)}, u32[]{:S(2)}) collective-permute-start(f32[2,18,1,512]{3,0,2,1:T(2,128)S(1)} %copy.167), channel_id=1, source_target_pairs={{1,0},{2,1},{3,2},{5,4},{6,5},{7,6},{9,8},{10,9},{11,10},{13,12},{... | collective-permute-start | bytes 221192 | tf_op jit(solution)/shard_map/ppermute | solution.py:18
  12.6 52.2 %collective-permute-start.2 = (f32[2,18,1,512]{3,0,2,1:T(2,128)S(1)}, f32[2,18,1,512]{3,0,2,1:T(2,128)S(1)}, u32[]{:S(2)}, u32[]{:S(2)}) collective-permute-start(f32[2,18,1,512]{3,0,2,1:T(2,128)S(1)} %copy.166), channel_id=1, source_target_pairs={{0,1},{1,2},{2,3},{4,5},{5,6},{6,7},{8,9},{9,10},{10,11},{12,13},{... | collective-permute-start | bytes 221192 | tf_op jit(solution)/shard_map/ppermute | solution.py:15
  65.4 1.2 copy-start.2
  70.4 4.4 %collective-permute-start.4 = (f32[1,32,512]{2,1,0:T(8,128)S(1)}, f32[1,32,512]{2,1,0:T(8,128)S(1)}, u32[]{:S(2)}, u32[]{:S(2)}) collective-permute-start(f32[1,32,512]{2,1,0:T(8,128)S(1)} %get-tuple-element.35), channel_id=1, source_target_pairs={{0,4},{4,8},{8,12},{12,16},{16,20},{20,24},{24,28},{1,5},{5,9},{9,... | collective-permute-start | bytes 196616 | tf_op jit(solution)/shard_map/ppermute | solution.py:15
  72.8 5.6 %collective-permute-start.5 = (f32[1,32,512]{2,1,0:T(8,128)S(1)}, f32[1,32,512]{2,1,0:T(8,128)S(1)}, u32[]{:S(2)}, u32[]{:S(2)}) collective-permute-start(f32[1,32,512]{2,1,0:T(8,128)S(1)} %get-tuple-element.36), channel_id=1, source_target_pairs={{4,0},{8,4},{12,8},{16,12},{20,16},{24,20},{28,24},{5,1},{9,5},{13... | collective-permute-start | bytes 196616 | tf_op jit(solution)/shard_map/ppermute | solution.py:18
  78.4 9.3 %collective-permute-start.6 = (f32[18,1,512]{2,1,0:T(1,128)S(1)}, f32[18,1,512]{2,1,0:T(1,128)S(1)}, u32[]{:S(2)}, u32[]{:S(2)}) collective-permute-start(f32[18,1,512]{2,1,0:T(1,128)S(1)} %get-tuple-element.31), channel_id=1, source_target_pairs={{0,1},{1,2},{2,3},{4,5},{5,6},{6,7},{8,9},{9,10},{10,11},{12,13},{... | collective-permute-start | bytes 110600 | tf_op jit(solution)/shard_map/ppermute | solution.py:15
  81.7 6.1 %collective-permute-start.7 = (f32[18,1,512]{2,1,0:T(1,128)S(1)}, f32[18,1,512]{2,1,0:T(1,128)S(1)}, u32[]{:S(2)}, u32[]{:S(2)}) collective-permute-start(f32[18,1,512]{2,1,0:T(1,128)S(1)} %get-tuple-element.32), channel_id=1, source_target_pairs={{1,0},{2,1},{3,2},{5,4},{6,5},{7,6},{9,8},{10,9},{11,10},{13,12},{... | collective-permute-start | bytes 110600 | tf_op jit(solution)/shard_map/ppermute | solution.py:18
  83.0 17.1 %collective-permute-start.12 = (f32[1,8,128]{2,1,0:T(8,128)S(1)}, f32[1,8,128]{2,1,0:T(8,128)S(1)}, u32[]{:S(2)}, u32[]{:S(2)}) collective-permute-start(f32[1,8,128]{2,1,0:T(8,128)S(1)} %get-tuple-element.67), channel_id=1, source_target_pairs={{0,4},{4,8},{8,12},{12,16},{16,20},{20,24},{24,28},{1,5},{5,9},{9,... | collective-permute-start | bytes 12296 | tf_op jit(solution)/shard_map/ppermute | solution.py:15
  85.1 14.9 %collective-permute-start.13 = (f32[1,8,128]{2,1,0:T(8,128)S(1)}, f32[1,8,128]{2,1,0:T(8,128)S(1)}, u32[]{:S(2)}, u32[]{:S(2)}) collective-permute-start(f32[1,8,128]{2,1,0:T(8,128)S(1)} %get-tuple-element.68), channel_id=1, source_target_pairs={{4,0},{8,4},{12,8},{16,12},{20,16},{24,20},{28,24},{5,1},{9,5},{13... | collective-permute-start | bytes 12296 | tf_op jit(solution)/shard_map/ppermute | solution.py:18
  93.5 12.7 %collective-permute-start.8 = (f32[1,32,512]{2,1,0:T(8,128)S(1)}, f32[1,32,512]{2,1,0:T(8,128)S(1)}, u32[]{:S(2)}, u32[]{:S(2)}) collective-permute-start(f32[1,32,512]{2,1,0:T(8,128)S(1)} %get-tuple-element.33), channel_id=1, source_target_pairs={{0,4},{4,8},{8,12},{12,16},{16,20},{20,24},{24,28},{1,5},{5,9},{9,... | collective-permute-start | bytes 196616 | tf_op jit(solution)/shard_map/ppermute | solution.py:15
  96.5 9.8 %collective-permute-start.9 = (f32[1,32,512]{2,1,0:T(8,128)S(1)}, f32[1,32,512]{2,1,0:T(8,128)S(1)}, u32[]{:S(2)}, u32[]{:S(2)}) collective-permute-start(f32[1,32,512]{2,1,0:T(8,128)S(1)} %get-tuple-element.34), channel_id=1, source_target_pairs={{4,0},{8,4},{12,8},{16,12},{20,16},{24,20},{28,24},{5,1},{9,5},{13... | collective-permute-start | bytes 196616 | tf_op jit(solution)/shard_map/ppermute | solution.py:18
  100.1 11.1 %collective-permute-start.15 = (f32[6,1,128]{2,1,0:T(1,128)S(1)}, f32[6,1,128]{2,1,0:T(1,128)S(1)}, u32[]{:S(2)}, u32[]{:S(2)}) collective-permute-start(f32[6,1,128]{2,1,0:T(1,128)S(1)} %get-tuple-element.51), channel_id=1, source_target_pairs={{1,0},{2,1},{3,2},{5,4},{6,5},{7,6},{9,8},{10,9},{11,10},{13,12},{... | collective-permute-start | bytes 9224 | tf_op jit(solution)/shard_map/ppermute | solution.py:18
  101.4 9.9 %collective-permute-start.14 = (f32[6,1,128]{2,1,0:T(1,128)S(1)}, f32[6,1,128]{2,1,0:T(1,128)S(1)}, u32[]{:S(2)}, u32[]{:S(2)}) collective-permute-start(f32[6,1,128]{2,1,0:T(1,128)S(1)} %get-tuple-element.52), channel_id=1, source_target_pairs={{0,1},{1,2},{2,3},{4,5},{5,6},{6,7},{8,9},{9,10},{10,11},{12,13},{... | collective-permute-start | bytes 9224 | tf_op jit(solution)/shard_map/ppermute | solution.py:15
  106.4 5.0 %collective-permute-start.10 = (f32[18,1,512]{2,1,0:T(1,128)S(1)}, f32[18,1,512]{2,1,0:T(1,128)S(1)}, u32[]{:S(2)}, u32[]{:S(2)}) collective-permute-start(f32[18,1,512]{2,1,0:T(1,128)S(1)} %get-tuple-element.29), channel_id=1, source_target_pairs={{0,1},{1,2},{2,3},{4,5},{5,6},{6,7},{8,9},{9,10},{10,11},{12,13},{... | collective-permute-start | bytes 110600 | tf_op jit(solution)/shard_map/ppermute | solution.py:15
  109.7 4.7 %collective-permute-start.11 = (f32[18,1,512]{2,1,0:T(1,128)S(1)}, f32[18,1,512]{2,1,0:T(1,128)S(1)}, u32[]{:S(2)}, u32[]{:S(2)}) collective-permute-start(f32[18,1,512]{2,1,0:T(1,128)S(1)} %get-tuple-element.30), channel_id=1, source_target_pairs={{1,0},{2,1},{3,2},{5,4},{6,5},{7,6},{9,8},{10,9},{11,10},{13,12},{... | collective-permute-start | bytes 110600 | tf_op jit(solution)/shard_map/ppermute | solution.py:18
  168.1 8.5 %collective-permute-start.16 = (f32[1,8,128]{2,1,0:T(8,128)S(1)}, f32[1,8,128]{2,1,0:T(8,128)S(1)}, u32[]{:S(2)}, u32[]{:S(2)}) collective-permute-start(f32[1,8,128]{2,1,0:T(8,128)S(1)} %get-tuple-element.65), channel_id=1, source_target_pairs={{0,4},{4,8},{8,12},{12,16},{16,20},{20,24},{24,28},{1,5},{5,9},{9,... | collective-permute-start | bytes 12296 | tf_op jit(solution)/shard_map/ppermute | solution.py:15
  172.2 5.2 %collective-permute-start.17 = (f32[1,8,128]{2,1,0:T(8,128)S(1)}, f32[1,8,128]{2,1,0:T(8,128)S(1)}, u32[]{:S(2)}, u32[]{:S(2)}) collective-permute-start(f32[1,8,128]{2,1,0:T(8,128)S(1)} %get-tuple-element.66), channel_id=1, source_target_pairs={{4,0},{8,4},{12,8},{16,12},{20,16},{24,20},{28,24},{5,1},{9,5},{13... | collective-permute-start | bytes 12296 | tf_op jit(solution)/shard_map/ppermute | solution.py:18
  177.4 4.5 %collective-permute-start.18 = (f32[6,1,128]{2,1,0:T(1,128)S(1)}, f32[6,1,128]{2,1,0:T(1,128)S(1)}, u32[]{:S(2)}, u32[]{:S(2)}) collective-permute-start(f32[6,1,128]{2,1,0:T(1,128)S(1)} %get-tuple-element.49), channel_id=1, source_target_pairs={{0,1},{1,2},{2,3},{4,5},{5,6},{6,7},{8,9},{9,10},{10,11},{12,13},{... | collective-permute-start | bytes 9224 | tf_op jit(solution)/shard_map/ppermute | solution.py:15
  180.6 4.3 %collective-permute-start.19 = (f32[6,1,128]{2,1,0:T(1,128)S(1)}, f32[6,1,128]{2,1,0:T(1,128)S(1)}, u32[]{:S(2)}, u32[]{:S(2)}) collective-permute-start(f32[6,1,128]{2,1,0:T(1,128)S(1)} %get-tuple-element.50), channel_id=1, source_target_pairs={{1,0},{2,1},{3,2},{5,4},{6,5},{7,6},{9,8},{10,9},{11,10},{13,12},{... | collective-permute-start | bytes 9224 | tf_op jit(solution)/shard_map/ppermute | solution.py:18
  185.2 8.4 %collective-permute-start.20 = (f32[1,8,128]{2,1,0:T(8,128)S(1)}, f32[1,8,128]{2,1,0:T(8,128)S(1)}, u32[]{:S(2)}, u32[]{:S(2)}) collective-permute-start(f32[1,8,128]{2,1,0:T(8,128)S(1)} %get-tuple-element.63), channel_id=1, source_target_pairs={{0,4},{4,8},{8,12},{12,16},{16,20},{20,24},{24,28},{1,5},{5,9},{9,... | collective-permute-start | bytes 12296 | tf_op jit(solution)/shard_map/ppermute | solution.py:15
  188.3 6.1 %collective-permute-start.21 = (f32[1,8,128]{2,1,0:T(8,128)S(1)}, f32[1,8,128]{2,1,0:T(8,128)S(1)}, u32[]{:S(2)}, u32[]{:S(2)}) collective-permute-start(f32[1,8,128]{2,1,0:T(8,128)S(1)} %get-tuple-element.64), channel_id=1, source_target_pairs={{4,0},{8,4},{12,8},{16,12},{20,16},{24,20},{28,24},{5,1},{9,5},{13... | collective-permute-start | bytes 12296 | tf_op jit(solution)/shard_map/ppermute | solution.py:18
  194.4 2.9 %collective-permute-start.22 = (f32[6,1,128]{2,1,0:T(1,128)S(1)}, f32[6,1,128]{2,1,0:T(1,128)S(1)}, u32[]{:S(2)}, u32[]{:S(2)}) collective-permute-start(f32[6,1,128]{2,1,0:T(1,128)S(1)} %get-tuple-element.47), channel_id=1, source_target_pairs={{0,1},{1,2},{2,3},{4,5},{5,6},{6,7},{8,9},{9,10},{10,11},{12,13},{... | collective-permute-start | bytes 9224 | tf_op jit(solution)/shard_map/ppermute | solution.py:15
  196.0 4.3 %collective-permute-start.23 = (f32[6,1,128]{2,1,0:T(1,128)S(1)}, f32[6,1,128]{2,1,0:T(1,128)S(1)}, u32[]{:S(2)}, u32[]{:S(2)}) collective-permute-start(f32[6,1,128]{2,1,0:T(1,128)S(1)} %get-tuple-element.48), channel_id=1, source_target_pairs={{1,0},{2,1},{3,2},{5,4},{6,5},{7,6},{9,8},{10,9},{11,10},{13,12},{... | collective-permute-start | bytes 9224 | tf_op jit(solution)/shard_map/ppermute | solution.py:18
  200.6 8.4 %collective-permute-start.24 = (f32[1,8,128]{2,1,0:T(8,128)S(1)}, f32[1,8,128]{2,1,0:T(8,128)S(1)}, u32[]{:S(2)}, u32[]{:S(2)}) collective-permute-start(f32[1,8,128]{2,1,0:T(8,128)S(1)} %get-tuple-element.61), channel_id=1, source_target_pairs={{0,4},{4,8},{8,12},{12,16},{16,20},{20,24},{24,28},{1,5},{5,9},{9,... | collective-permute-start | bytes 12296 | tf_op jit(solution)/shard_map/ppermute | solution.py:15
  202.8 7.0 %collective-permute-start.25 = (f32[1,8,128]{2,1,0:T(8,128)S(1)}, f32[1,8,128]{2,1,0:T(8,128)S(1)}, u32[]{:S(2)}, u32[]{:S(2)}) collective-permute-start(f32[1,8,128]{2,1,0:T(8,128)S(1)} %get-tuple-element.62), channel_id=1, source_target_pairs={{4,0},{8,4},{12,8},{16,12},{20,16},{24,20},{28,24},{5,1},{9,5},{13... | collective-permute-start | bytes 12296 | tf_op jit(solution)/shard_map/ppermute | solution.py:18
  209.8 2.9 %collective-permute-start.26 = (f32[6,1,128]{2,1,0:T(1,128)S(1)}, f32[6,1,128]{2,1,0:T(1,128)S(1)}, u32[]{:S(2)}, u32[]{:S(2)}) collective-permute-start(f32[6,1,128]{2,1,0:T(1,128)S(1)} %get-tuple-element.45), channel_id=1, source_target_pairs={{0,1},{1,2},{2,3},{4,5},{5,6},{6,7},{8,9},{9,10},{10,11},{12,13},{... | collective-permute-start | bytes 9224 | tf_op jit(solution)/shard_map/ppermute | solution.py:15
  211.5 4.3 %collective-permute-start.27 = (f32[6,1,128]{2,1,0:T(1,128)S(1)}, f32[6,1,128]{2,1,0:T(1,128)S(1)}, u32[]{:S(2)}, u32[]{:S(2)}) collective-permute-start(f32[6,1,128]{2,1,0:T(1,128)S(1)} %get-tuple-element.46), channel_id=1, source_target_pairs={{1,0},{2,1},{3,2},{5,4},{6,5},{7,6},{9,8},{10,9},{11,10},{13,12},{... | collective-permute-start | bytes 9224 | tf_op jit(solution)/shard_map/ppermute | solution.py:18
  216.0 8.4 %collective-permute-start.28 = (f32[1,8,128]{2,1,0:T(8,128)S(1)}, f32[1,8,128]{2,1,0:T(8,128)S(1)}, u32[]{:S(2)}, u32[]{:S(2)}) collective-permute-start(f32[1,8,128]{2,1,0:T(8,128)S(1)} %get-tuple-element.59), channel_id=1, source_target_pairs={{0,4},{4,8},{8,12},{12,16},{16,20},{20,24},{24,28},{1,5},{5,9},{9,... | collective-permute-start | bytes 12296 | tf_op jit(solution)/shard_map/ppermute | solution.py:15
  218.0 7.3 %collective-permute-start.29 = (f32[1,8,128]{2,1,0:T(8,128)S(1)}, f32[1,8,128]{2,1,0:T(8,128)S(1)}, u32[]{:S(2)}, u32[]{:S(2)}) collective-permute-start(f32[1,8,128]{2,1,0:T(8,128)S(1)} %get-tuple-element.60), channel_id=1, source_target_pairs={{4,0},{8,4},{12,8},{16,12},{20,16},{24,20},{28,24},{5,1},{9,5},{13... | collective-permute-start | bytes 12296 | tf_op jit(solution)/shard_map/ppermute | solution.py:18
  225.3 2.9 %collective-permute-start.30 = (f32[6,1,128]{2,1,0:T(1,128)S(1)}, f32[6,1,128]{2,1,0:T(1,128)S(1)}, u32[]{:S(2)}, u32[]{:S(2)}) collective-permute-start(f32[6,1,128]{2,1,0:T(1,128)S(1)} %get-tuple-element.43), channel_id=1, source_target_pairs={{0,1},{1,2},{2,3},{4,5},{5,6},{6,7},{8,9},{9,10},{10,11},{12,13},{... | collective-permute-start | bytes 9224 | tf_op jit(solution)/shard_map/ppermute | solution.py:15
  226.9 4.3 %collective-permute-start.31 = (f32[6,1,128]{2,1,0:T(1,128)S(1)}, f32[6,1,128]{2,1,0:T(1,128)S(1)}, u32[]{:S(2)}, u32[]{:S(2)}) collective-permute-start(f32[6,1,128]{2,1,0:T(1,128)S(1)} %get-tuple-element.44), channel_id=1, source_target_pairs={{1,0},{2,1},{3,2},{5,4},{6,5},{7,6},{9,8},{10,9},{11,10},{13,12},{... | collective-permute-start | bytes 9224 | tf_op jit(solution)/shard_map/ppermute | solution.py:18
  231.5 8.4 %collective-permute-start.32 = (f32[1,8,128]{2,1,0:T(8,128)S(1)}, f32[1,8,128]{2,1,0:T(8,128)S(1)}, u32[]{:S(2)}, u32[]{:S(2)}) collective-permute-start(f32[1,8,128]{2,1,0:T(8,128)S(1)} %get-tuple-element.57), channel_id=1, source_target_pairs={{0,4},{4,8},{8,12},{12,16},{16,20},{20,24},{24,28},{1,5},{5,9},{9,... | collective-permute-start | bytes 12296 | tf_op jit(solution)/shard_map/ppermute | solution.py:15
  233.4 7.3 %collective-permute-start.33 = (f32[1,8,128]{2,1,0:T(8,128)S(1)}, f32[1,8,128]{2,1,0:T(8,128)S(1)}, u32[]{:S(2)}, u32[]{:S(2)}) collective-permute-start(f32[1,8,128]{2,1,0:T(8,128)S(1)} %get-tuple-element.58), channel_id=1, source_target_pairs={{4,0},{8,4},{12,8},{16,12},{20,16},{24,20},{28,24},{5,1},{9,5},{13... | collective-permute-start | bytes 12296 | tf_op jit(solution)/shard_map/ppermute | solution.py:18
  240.7 2.9 %collective-permute-start.34 = (f32[6,1,128]{2,1,0:T(1,128)S(1)}, f32[6,1,128]{2,1,0:T(1,128)S(1)}, u32[]{:S(2)}, u32[]{:S(2)}) collective-permute-start(f32[6,1,128]{2,1,0:T(1,128)S(1)} %get-tuple-element.41), channel_id=1, source_target_pairs={{0,1},{1,2},{2,3},{4,5},{5,6},{6,7},{8,9},{9,10},{10,11},{12,13},{... | collective-permute-start | bytes 9224 | tf_op jit(solution)/shard_map/ppermute | solution.py:15
  242.3 4.3 %collective-permute-start.35 = (f32[6,1,128]{2,1,0:T(1,128)S(1)}, f32[6,1,128]{2,1,0:T(1,128)S(1)}, u32[]{:S(2)}, u32[]{:S(2)}) collective-permute-start(f32[6,1,128]{2,1,0:T(1,128)S(1)} %get-tuple-element.42), channel_id=1, source_target_pairs={{1,0},{2,1},{3,2},{5,4},{6,5},{7,6},{9,8},{10,9},{11,10},{13,12},{... | collective-permute-start | bytes 9224 | tf_op jit(solution)/shard_map/ppermute | solution.py:18
  246.9 8.4 %collective-permute-start.36 = (f32[1,8,128]{2,1,0:T(8,128)S(1)}, f32[1,8,128]{2,1,0:T(8,128)S(1)}, u32[]{:S(2)}, u32[]{:S(2)}) collective-permute-start(f32[1,8,128]{2,1,0:T(8,128)S(1)} %get-tuple-element.55), channel_id=1, source_target_pairs={{0,4},{4,8},{8,12},{12,16},{16,20},{20,24},{24,28},{1,5},{5,9},{9,... | collective-permute-start | bytes 12296 | tf_op jit(solution)/shard_map/ppermute | solution.py:15
  248.8 7.3 %collective-permute-start.37 = (f32[1,8,128]{2,1,0:T(8,128)S(1)}, f32[1,8,128]{2,1,0:T(8,128)S(1)}, u32[]{:S(2)}, u32[]{:S(2)}) collective-permute-start(f32[1,8,128]{2,1,0:T(8,128)S(1)} %get-tuple-element.56), channel_id=1, source_target_pairs={{4,0},{8,4},{12,8},{16,12},{20,16},{24,20},{28,24},{5,1},{9,5},{13... | collective-permute-start | bytes 12296 | tf_op jit(solution)/shard_map/ppermute | solution.py:18
  256.1 2.9 %collective-permute-start.38 = (f32[6,1,128]{2,1,0:T(1,128)S(1)}, f32[6,1,128]{2,1,0:T(1,128)S(1)}, u32[]{:S(2)}, u32[]{:S(2)}) collective-permute-start(f32[6,1,128]{2,1,0:T(1,128)S(1)} %get-tuple-element.39), channel_id=1, source_target_pairs={{0,1},{1,2},{2,3},{4,5},{5,6},{6,7},{8,9},{9,10},{10,11},{12,13},{... | collective-permute-start | bytes 9224 | tf_op jit(solution)/shard_map/ppermute | solution.py:15
  257.8 4.3 %collective-permute-start.39 = (f32[6,1,128]{2,1,0:T(1,128)S(1)}, f32[6,1,128]{2,1,0:T(1,128)S(1)}, u32[]{:S(2)}, u32[]{:S(2)}) collective-permute-start(f32[6,1,128]{2,1,0:T(1,128)S(1)} %get-tuple-element.40), channel_id=1, source_target_pairs={{1,0},{2,1},{3,2},{5,4},{6,5},{7,6},{9,8},{10,9},{11,10},{13,12},{... | collective-permute-start | bytes 9224 | tf_op jit(solution)/shard_map/ppermute | solution.py:18
  262.3 8.4 %collective-permute-start.40 = (f32[1,8,128]{2,1,0:T(8,128)S(1)}, f32[1,8,128]{2,1,0:T(8,128)S(1)}, u32[]{:S(2)}, u32[]{:S(2)}) collective-permute-start(f32[1,8,128]{2,1,0:T(8,128)S(1)} %get-tuple-element.53), channel_id=1, source_target_pairs={{0,4},{4,8},{8,12},{12,16},{16,20},{20,24},{24,28},{1,5},{5,9},{9,... | collective-permute-start | bytes 12296 | tf_op jit(solution)/shard_map/ppermute | solution.py:15
  264.3 7.3 %collective-permute-start.41 = (f32[1,8,128]{2,1,0:T(8,128)S(1)}, f32[1,8,128]{2,1,0:T(8,128)S(1)}, u32[]{:S(2)}, u32[]{:S(2)}) collective-permute-start(f32[1,8,128]{2,1,0:T(8,128)S(1)} %get-tuple-element.54), channel_id=1, source_target_pairs={{4,0},{8,4},{12,8},{16,12},{20,16},{24,20},{28,24},{5,1},{9,5},{13... | collective-permute-start | bytes 12296 | tf_op jit(solution)/shard_map/ppermute | solution.py:18
  271.6 2.9 %collective-permute-start.42 = (f32[6,1,128]{2,1,0:T(1,128)S(1)}, f32[6,1,128]{2,1,0:T(1,128)S(1)}, u32[]{:S(2)}, u32[]{:S(2)}) collective-permute-start(f32[6,1,128]{2,1,0:T(1,128)S(1)} %get-tuple-element.37), channel_id=1, source_target_pairs={{0,1},{1,2},{2,3},{4,5},{5,6},{6,7},{8,9},{9,10},{10,11},{12,13},{... | collective-permute-start | bytes 9224 | tf_op jit(solution)/shard_map/ppermute | solution.py:15
  273.2 4.3 %collective-permute-start.43 = (f32[6,1,128]{2,1,0:T(1,128)S(1)}, f32[6,1,128]{2,1,0:T(1,128)S(1)}, u32[]{:S(2)}, u32[]{:S(2)}) collective-permute-start(f32[6,1,128]{2,1,0:T(1,128)S(1)} %get-tuple-element.38), channel_id=1, source_target_pairs={{1,0},{2,1},{3,2},{5,4},{6,5},{7,6},{9,8},{10,9},{11,10},{13,12},{... | collective-permute-start | bytes 9224 | tf_op jit(solution)/shard_map/ppermute | solution.py:18
where the time goes:
time: 290 us; the launch traced here: 285 us
  starting transfers between devices  123 us (42%)
  local copies, waits for them, and re-layouts  79.1 us (27%)
  other arithmetic  44.1 us (15%)
  waiting for transfers between devices  37.8 us (13%)
    reshape x2, local copies, waits for them, and re-layouts, block_mean(): field.reshape(sx // 4, 4, sy // 4, 4, sz // 4, 4).mean(axis=(1, 3, 5))  71.9 us
    ppermute x22, starting transfers between devices, extended(): lax.ppermute(lax.slice_in_dim(block, 0, width, axis=dim), axis, backward)  66.3 us
    ppermute x22, starting transfers between devices, extended(): lax.ppermute(lax.slice_in_dim(block, block.shape[dim] - width, None, axis...  56.5 us
    ppermute x22, waiting for transfers between devices, extended(): lax.ppermute(lax.slice_in_dim(block, 0, width, axis=dim), axis, backward)  37.7 us
    reduce_sum x2, other arithmetic, block_mean(): field.reshape(sx // 4, 4, sy // 4, 4, sz // 4, 4).mean(axis=(1, 3, 5))  24.4 us
    add x2, other arithmetic, per_device(): fine + 2.0 / 3.0 * (right_side - stencil(fine, fine_padded, coefs)) / diag  8.71 us
  transfers between devices with their start and end apart: 44, of which 17 were waited for; matrix products, arithmetic and copies ran while one was open for 19% of the time, Pallas kernels for 0%

commit v1 on v0

v1 whole, which is shorter than its diff:
```python
import functools

import jax
import jax.numpy as jnp
from jax import lax
from jax.experimental import pallas as pl
from jax.experimental.pallas import tpu as pltpu
from jax.sharding import PartitionSpec as P

CHEB = 8
POOL = 4
MESH = pl.DeviceIdType.MESH


def chebyshev_factors():
    low, high = 0.05, 2.0
    theta = (high + low) / 2.0
    delta = (high - low) / 2.0
    sigma = theta / delta
    rho = 1.0 / sigma
    steps = []
    for _ in range(CHEB - 1):
        rho_next = 1.0 / (2.0 * sigma - rho)
        steps.append((rho_next * rho, 2.0 * rho_next / delta))
        rho = rho_next
    return 1.0 / theta, steps


def inverse(x):
    r = pl.reciprocal(x, approx=True)
    return r * (2.0 - x * r)


def face(a, b):
    m = a * b
    return (m + m) * inverse(a + b)


def edge_face(a, b):
    m = a * b
    s = a + b
    return jnp.where(m > 0, (m + m) * inverse(s), s)


def split(x):
    hi = x.astype(jnp.bfloat16)
    return hi, (x - hi.astype(jnp.float32)).astype(jnp.bfloat16)


def dot(a, b):
    return jnp.dot(a, b, preferred_element_type=jnp.float32)


def members(rows, cols, long_first):
    r = lax.broadcasted_iota(jnp.int32, (rows, cols), 0)
    c = lax.broadcasted_iota(jnp.int32, (rows, cols), 1)
    same = (r // POOL == c) if long_first else (r == c // POOL)
    return same.astype(jnp.float32).astype(jnp.bfloat16)


def pool(stack):
    g, rows, lanes = stack.shape
    flat = stack.reshape(g * rows, lanes)
    across = members(lanes, lanes // POOL, True)
    hi, lo = split(flat)
    m = dot(hi, across) + dot(lo, across)
    down = members(g * rows // POOL, g * rows, False)
    hi, lo = split(m)
    return (dot(down, hi) + dot(down, lo)) * (1.0 / POOL**3)


def cycle_kernel(
    nb, ng, f_hbm, b_hbm, p_hbm, fine_hbm, e_ref,
    V0, B, V1, V2, F, CX, CY, CZ, W, D, T, ysend, yrecv, yface, ygain,
    ACC, GB, GR, KX, KY, KZ, KW, DD,
    lsem, fsend, frecv, csend, crecv,
):
    nx, ny, nz = F.shape
    cx, cy, cz = nx // POOL, ny // POOL, nz // POOL
    hb, hg = (GB.shape[0] // cx - 1) // 2, (GB.shape[1] // cy - 1) // 2
    bx, gx = lax.axis_index("box"), lax.axis_index("group")

    def there(dx, dg):
        ok = (bx + dx >= 0) & (bx + dx < nb)
        return ok & (gx + dg >= 0) & (gx + dg < ng)

    offsets = [
        (dx, dg)
        for dg in range(-hg, hg + 1)
        for dx in range(-hb, hb + 1)
        if (dx, dg) != (0, 0)
    ]
    barrier = pltpu.get_barrier_semaphore()
    for dx, dg in offsets:
        @pl.when(there(dx, dg))
        def _():
            pl.semaphore_signal(
                barrier, inc=1, device_id={"box": bx + dx, "group": gx + dg}, device_id_type=MESH
            )

    inside = pl.ds(1, nx)
    load_b = pltpu.make_async_copy(b_hbm, B.at[inside], lsem.at[0])
    load_p = pltpu.make_async_copy(p_hbm, V0.at[inside], lsem.at[1])
    load_f = pltpu.make_async_copy(f_hbm, F, lsem.at[2])
    load_b.start()
    load_p.start()
    load_f.start()

    fields = [V0, B, V1, V2]
    goes = [(1, 0), (-1, 0), (0, 1), (0, -1)]

    def fine_copy(a, way):
        if way == 0:
            src = (p_hbm, b_hbm)[a].at[nx - 1] if a < 2 else fields[a].at[nx]
            dst = fields[a].at[0]
        elif way == 1:
            src = (p_hbm, b_hbm)[a].at[0] if a < 2 else fields[a].at[1]
            dst = fields[a].at[nx + 1]
        else:
            src, dst = ysend.at[a, 3 - way], yrecv.at[a, way - 2]
        dx, dg = goes[way]
        return pltpu.make_async_remote_copy(
            src_ref=src, dst_ref=dst, send_sem=fsend.at[a, way], recv_sem=frecv.at[a, way],
            device_id={"box": bx + dx, "group": gx + dg}, device_id_type=MESH,
        )

    def send(a, ways):
        for way in ways:
            @pl.when(there(*goes[way]))
            def _():
                fine_copy(a, way).start()

    def receive(a, ways):
        for way in ways:
            @pl.when(there(-goes[way][0], -goes[way][1]))
            def _():
                fine_copy(a, way).wait_recv()

    def coarse_copy(a, o):
        dx, dg = offsets[o]
        G = (GB, GR)[a]
        return pltpu.make_async_remote_copy(
            src_ref=G.at[pl.ds(hb * cx, cx), pl.ds(hg * cy, cy)],
            dst_ref=G.at[pl.ds((hb - dx) * cx, cx), pl.ds((hg - dg) * cy, cy)],
            send_sem=csend.at[a, o], recv_sem=crecv.at[a, o],
            device_id={"box": bx + dx, "group": gx + dg}, device_id_type=MESH,
        )

    def coarse_send(a):
        for o, (dx, dg) in enumerate(offsets):
            @pl.when(there(dx, dg))
            def _():
                coarse_copy(a, o).start()

    def coarse_receive(a):
        for o, (dx, dg) in enumerate(offsets):
            @pl.when(there(-dx, -dg))
            def _():
                coarse_copy(a, o).wait_recv()

    for way in (0, 1):
        @pl.when(jnp.logical_not(there(-goes[way][0], 0)))
        def _():
            for field in fields:
                field[way * (nx + 1)] = jnp.zeros((ny, nz), jnp.float32)
    for way in (2, 3):
        @pl.when(jnp.logical_not(there(0, -goes[way][1])))
        def _():
            for a in range(4):
                yrecv[a, way - 2] = jnp.zeros((nx, nz), jnp.float32)
    for dx, dg in offsets:
        @pl.when(jnp.logical_not(there(dx, dg)))
        def _():
            for G in (GB, GR):
                G[pl.ds((hb + dx) * cx, cx), pl.ds((hg + dg) * cy, cy)] = jnp.zeros(
                    (cx, cy, cz), jnp.float32
                )

    neighbours = 0
    for dx, dg in offsets:
        neighbours = neighbours + there(dx, dg).astype(jnp.int32)
    pl.semaphore_wait(barrier, neighbours)
    send(1, (0, 1))
    send(0, (0, 1))

    def pack(a):
        ysend[a, 0] = fields[a][pl.ds(1, nx), 0, :]
        ysend[a, 1] = fields[a][pl.ds(1, nx), ny - 1, :]

    load_b.wait()
    pack(1)
    send(1, (2, 3))
    load_p.wait()
    pack(0)
    send(0, (2, 3))
    load_f.wait()

    lane = lax.broadcasted_iota(jnp.int32, (ny, nz), 1)
    row = lax.broadcasted_iota(jnp.int32, (ny, nz), 0)
    low_row = lax.broadcasted_iota(jnp.int32, (8, nz), 0) == 0
    high_row = lax.broadcasted_iota(jnp.int32, (8, nz), 0) == 7

    def in_plane(v, ky, kz):
        s = kz * pltpu.roll(v, nz - 1, 1) + pltpu.roll(kz * v, 1, 1)
        return s + (ky * pltpu.roll(v, ny - 1, 0) + pltpu.roll(ky * v, 1, 0))

    def add_rows(t, low, high):
        return jnp.concatenate(
            [
                t[0:8] + jnp.where(low_row, low, 0.0),
                t[8 : ny - 8],
                t[ny - 8 : ny] + jnp.where(high_row, high, 0.0),
            ],
            axis=0,
        )

    def before_halo(i, first=False):
        b, p = B[i + 1], V0[i + 1]
        kz = jnp.where(lane == nz - 1, 0.0, face(b, pltpu.roll(b, nz - 1, 1)))
        ky = jnp.where(row == ny - 1, 0.0, face(b, pltpu.roll(b, ny - 1, 0)))
        CZ[i] = kz
        CY[i] = ky
        if not first:
            CX[i] = face(B[i], b)
        ends = jnp.where((lane == 0) | (lane == nz - 1), b, 0.0)
        D[i] = (kz + pltpu.roll(kz, 1, 1)) + (ky + pltpu.roll(ky, 1, 0)) + ends
        T[i] = F[i] + in_plane(p, ky, kz)

    before_halo(0, True)
    lax.fori_loop(1, nx, lambda i, c: (before_halo(i), c)[1], 0)

    def sum_b(g, c):
        s = B[POOL * g + 1]
        for k in range(1, POOL):
            s = s + B[POOL * g + 1 + k]
        ACC[g] = s
        return c

    lax.fori_loop(0, cx, sum_b, 0)
    center = (pl.ds(hb * cx, cx), pl.ds(hg * cy, cy))
    GB[center] = pool(ACC[...]).reshape(cx, cy, cz)
    coarse_send(0)

    receive(1, (0, 1, 2, 3))
    CX[0] = edge_face(B[0], B[1])
    CX[nx] = edge_face(B[nx], B[nx + 1])
    for side in (0, 1):
        yface[side] = edge_face(ysend[1, side], yrecv[1, side])
    receive(0, (0, 1, 2, 3))

    def gains(a):
        for side in (0, 1):
            ygain[side] = yface[side] * yrecv[a, side]

    gains(0)

    def first_sweep(i):
        at = pl.ds(i, 1)
        k0, k1 = CX[i], CX[i + 1]
        d = add_rows(D[i] + (k0 + k1), yface[0, at, :], yface[1, at, :])
        D[i] = d
        w = (2.0 / 3.0) * inverse(d)
        W[i] = w
        t = T[i] + (k0 * V0[i] + k1 * V0[i + 2])
        t = add_rows(t, ygain[0, at, :], ygain[1, at, :])
        V1[i + 1] = (1.0 / 3.0) * V0[i + 1] + w * t

    def both_ends(step):
        lax.fori_loop(0, 2, lambda j, c: (step(j * (nx - 1)), c)[1], 0)

    def between(step):
        lax.fori_loop(1, nx - 1, lambda i, c: (step(i), c)[1], 0)

    both_ends(first_sweep)
    send(2, (0, 1))
    between(first_sweep)
    pack(2)
    send(2, (2, 3))

    def total(V, i):
        v = V[i + 1]
        x = CX[i] * V[i] + CX[i + 1] * V[i + 2]
        return v, F[i] + x + in_plane(v, CY[i], CZ[i])

    def second_sweep(i):
        v, t = total(V1, i)
        V2[i + 1] = (1.0 / 3.0) * v + W[i] * t

    between(second_sweep)
    receive(2, (0, 1))
    both_ends(second_sweep)
    receive(2, (2, 3))
    gains(2)

    bottom, top = pl.ds(0, 8), pl.ds(ny - 8, 8)

    def second_rows(i, c):
        at = pl.ds(i, 1)
        V2[i + 1, bottom, :] += jnp.where(low_row, W[i, bottom, :] * ygain[0, at, :], 0.0)
        V2[i + 1, top, :] += jnp.where(high_row, W[i, top, :] * ygain[1, at, :], 0.0)
        return c

    lax.fori_loop(0, nx, second_rows, 0)
    send(3, (0, 1))
    pack(3)
    send(3, (2, 3))
    store = pltpu.make_async_copy(V2.at[inside], fine_hbm, lsem.at[3])
    store.start()

    ACC[...] = jnp.zeros_like(ACC)

    def residual(i):
        v, t = total(V2, i)
        ACC[i // POOL] += t - D[i] * v

    between(residual)

    coarse_receive(0)
    gb = GB[...]
    ex, ey, ez = gb.shape
    clane = lax.broadcasted_iota(jnp.int32, gb.shape, 2)
    kx = edge_face(gb[:-1], gb[1:])
    ky = edge_face(gb, pltpu.roll(gb, ey - 1, 1))
    kz = jnp.where(clane == ez - 1, 0.0, edge_face(gb, pltpu.roll(gb, ez - 1, 2)))
    KX[...] = kx
    KY[...] = ky
    KZ[...] = kz
    ends = jnp.where((clane == 0) | (clane == ez - 1), gb, 0.0)
    d = (kz + pltpu.roll(kz, 1, 2)) + (ky + pltpu.roll(ky, 1, 1)) + ends
    d = d[1:-1] + (kx[:-1] + kx[1:])
    KW[pl.ds(1, ex - 2)] = jnp.where(gb[1:-1] > 0, inverse(d), 0.0)

    receive(3, (0, 1))
    both_ends(residual)
    receive(3, (2, 3))
    gains(3)

    def residual_rows(i, c):
        at, g = pl.ds(i, 1), i // POOL
        ACC[g, bottom, :] += jnp.where(low_row, ygain[0, at, :], 0.0)
        ACC[g, top, :] += jnp.where(high_row, ygain[1, at, :], 0.0)
        return c

    lax.fori_loop(0, nx, residual_rows, 0)
    GR[center] = pool(ACC[...]).reshape(cx, cy, cz)
    coarse_send(1)
    coarse_receive(1)

    start, steps = chebyshev_factors()
    lo, hi = 1, ex - 1
    q = GR[pl.ds(lo, hi - lo)] * KW[pl.ds(lo, hi - lo)] * 16.0
    d = q * start
    DD[pl.ds(lo, hi - lo)] = d
    e = DD[center]
    for decay, gain in steps:
        lo, hi = lo + 1, hi - 1
        span = pl.ds(lo, hi - lo)
        v = DD[span]
        ky, kz = KY[span], KZ[span]
        s = KX[pl.ds(lo - 1, hi - lo)] * DD[pl.ds(lo - 1, hi - lo)]
        s = s + KX[span] * DD[pl.ds(lo + 1, hi - lo)]
        s = s + (ky * pltpu.roll(v, ey - 1, 1) + pltpu.roll(ky * v, 1, 1))
        s = s + (kz * pltpu.roll(v, ez - 1, 2) + pltpu.roll(kz * v, 1, 2))
        q = q[1:-1] - v + KW[span] * s
        DD[span] = decay * v + gain * q
        e = e + DD[center]
    e_ref[...] = e.reshape(cx * cy, cz)

    for a in range(4):
        for way in range(4):
            @pl.when(there(*goes[way]))
            def _():
                fine_copy(a, way).wait_send()
    for a in range(2):
        for o, (dx, dg) in enumerate(offsets):
            @pl.when(there(dx, dg))
            def _():
                coarse_copy(a, o).wait_send()
    store.wait()


def expand_kernel(fine_ref, e_ref, out_ref):
    planes, ny, nz = fine_ref.shape
    cy, cz = e_ref.shape
    across = members(cz, nz, False)
    hi, lo = split(e_ref[...])
    wide = dot(hi, across) + dot(lo, across)
    down = members(ny, cy, True)
    hi, lo = split(wide)
    tall = dot(down, hi) + dot(down, lo)
    for k in range(planes):
        out_ref[k] = fine_ref[k] + tall


def per_device(nb, ng, right_side, inv_density, pressure):
    nx, ny, nz = right_side.shape
    cx, cy, cz = nx // POOL, ny // POOL, nz // POOL
    hb, hg = -(-CHEB // cx), -(-CHEB // cy)
    ex, ey = (2 * hb + 1) * cx, (2 * hg + 1) * cy
    count = (2 * hb + 1) * (2 * hg + 1) - 1
    f32 = jnp.float32
    block = pltpu.VMEM((nx, ny, nz), f32)
    padded = pltpu.VMEM((nx + 2, ny, nz), f32)
    coarse = pltpu.VMEM((ex, ey, cz), f32)
    dma = pltpu.SemaphoreType.DMA
    hbm = pl.BlockSpec(memory_space=pl.ANY)
    fine, e = pl.pallas_call(
        functools.partial(cycle_kernel, nb, ng),
        out_shape=(
            jax.ShapeDtypeStruct((nx, ny, nz), f32),
            jax.ShapeDtypeStruct((cx * cy, cz), f32),
        ),
        in_specs=[hbm] * 3,
        out_specs=(hbm, pl.BlockSpec(memory_space=pltpu.VMEM)),
        scratch_shapes=[
            padded, padded, padded, padded,
            block,
            pltpu.VMEM((nx + 1, ny, nz), f32),
            block, block, block, block, block,
            pltpu.VMEM((4, 2, nx, nz), f32),
            pltpu.VMEM((4, 2, nx, nz), f32),
            pltpu.VMEM((2, nx, nz), f32),
            pltpu.VMEM((2, nx, nz), f32),
            pltpu.VMEM((cx, ny, nz), f32),
            coarse, coarse,
            pltpu.VMEM((ex - 1, ey, cz), f32),
            coarse, coarse, coarse, coarse,
            dma((4,)), dma((4, 4)), dma((4, 4)), dma((2, count)), dma((2, count)),
        ],
        compiler_params=pltpu.CompilerParams(
            collective_id=0, has_side_effects=True, vmem_limit_bytes=40 * 1024 * 1024
        ),
        name="cycle",
    )(right_side, inv_density, pressure)
    return pl.pallas_call(
        expand_kernel,
        grid=(cx,),
        out_shape=jax.ShapeDtypeStruct((nx, ny, nz), f32),
        in_specs=[
            pl.BlockSpec((POOL, ny, nz), lambda g: (g, 0, 0)),
            pl.BlockSpec((cy, cz), lambda g: (g, 0)),
        ],
        out_specs=pl.BlockSpec((POOL, ny, nz), lambda g: (g, 0, 0)),
        name="expand",
    )(fine, e)


def solution(mesh):
    spec = P("box", "group", None)
    return jax.shard_map(
        functools.partial(per_device, mesh.shape["box"], mesh.shape["group"]),
        mesh=mesh,
        in_specs=(spec, spec, spec),
        out_specs=spec,
        check_vma=False,
    )
```

time: 290 us -> 33.5 us (0.12); the launches traced: 285 us -> 33.2 us
  starting transfers between devices: 123 us -> 0 us
  local copies, waits for them, and re-layouts: 79.1 us -> 5.24 us
  other arithmetic: 44.1 us -> 0 us
  waiting for transfers between devices: 37.8 us -> 0 us
  Pallas kernels: 0 us -> 27.9 us
    ppermute x44 -> x0, starting transfers between devices: 123 us -> none  [the longest x22 66.3 us: extended(): lax.ppermute(lax.slice_in_dim(block, 0, width, axis=dim), axis, backward)]
    reshape x4 -> x0, local copies, waits for them, and re-layouts: 75.2 us -> none  [the longest x2 71.9 us: block_mean(): field.reshape(sx // 4, 4, sy // 4, 4, sz // 4, 4).mean(axis=(1, 3, 5))]
    ppermute x44 -> x0, waiting for transfers between devices: 37.8 us -> none  [the longest x22 37.7 us: extended(): lax.ppermute(lax.slice_in_dim(block, 0, width, axis=dim), axis, backward)]
    pallas_call x0 -> x2, Pallas kernels: none -> 27.9 us  [the longest x1 24 us: per_device(): pl.pallas_call(functools.partial(cycle_kernel, nb, ng), out_shape=(jax.Sh...]
    reduce_sum x2 -> x0, other arithmetic: 24.4 us -> none  [block_mean(): field.reshape(sx // 4, 4, sy // 4, 4, sz // 4, 4).mean(axis=(1, 3, 5))]
    add x10 -> x0, other arithmetic: 10.5 us -> none  [the longest x2 8.71 us: per_device(): fine + 2.0 / 3.0 * (right_side - stencil(fine, fine_padded, coefs)) / diag]
    sub x1 -> x0, other arithmetic: 4.61 us -> none  [per_device(): res = right_side - stencil(fine, fine_padded, coefs)]
    unnamed x8 -> x10, local copies, waits for them, and re-layouts: 1.02 us -> 5.24 us
  transfers between devices with their start and end apart: 44 -> 0, of which waited for: 17 -> 0; matrix products, arithmetic and copies ran while one was open for 19% -> 0% of each run, Pallas kernels for 0% -> 0%
where the time goes in v1:
time: 33.5 us; the launch traced here: 33.2 us
  Pallas kernels  27.9 us (83%)
  local copies, waits for them, and re-layouts  5.24 us (16%)
    pallas_call x1, Pallas kernels, per_device(): pl.pallas_call(functools.partial(cycle_kernel, nb, ng), out_shape=(jax.Sh...  24 us
    unnamed x10, local copies, waits for them, and re-layouts  5.24 us
    pallas_call x1, Pallas kernels, per_device(): pl.pallas_call(expand_kernel, grid=(cx,), out_shape=jax.ShapeDtypeStruct(...  3.93 us

profile of v1, /device:TPU:5, one launch (start us, length us, event | category | flops | bytes accessed | tf_op | source)
XLA Modules:
  0.0 33.2 jit_solution(749579711463475492)
XLA Ops:
  0.0 0.0 copy-start
  0.0 1.2 %copy-done = f32[16,32,512]{2,1,0:T(8,128)S(1)} copy-done((f32[16,32,512]{2,1,0:T(8,128)S(1)}, f32[16,32,512]{2,1,0:T(8,128)}, u32[]{:S(2)}) %copy-start) | copy-done | bytes 1048600
  1.2 0.0 copy-start.1
  1.2 1.2 %copy-done.1 = f32[16,32,512]{2,1,0:T(8,128)S(1)} copy-done((f32[16,32,512]{2,1,0:T(8,128)S(1)}, f32[16,32,512]{2,1,0:T(8,128)}, u32[]{:S(2)}) %copy-start.1) | copy-done | bytes 1048600
  2.5 0.0 copy-start.2
  2.5 1.2 %copy-done.2 = f32[16,32,512]{2,1,0:T(8,128)S(1)} copy-done((f32[16,32,512]{2,1,0:T(8,128)S(1)}, f32[16,32,512]{2,1,0:T(8,128)}, u32[]{:S(2)}) %copy-start.2) | copy-done | bytes 1048600
  3.7 24.0 %cycle.1 = (f32[16,32,512]{2,1,0:T(8,128)S(1)}, f32[32,128]{1,0:T(8,128)S(1)}) custom-call(f32[16,32,512]{2,1,0:T(8,128)S(1)} %copy-done, f32[16,32,512]{2,1,0:T(8,128)S(1)} %copy-done.1, f32[16,32,512]{2,1,0:T(8,128)S(1)} %copy-done.2), custom_call_target="tpu_custom_call" | custom-call | tf_op jit(solution)/shard_map/cycle/pallas_call | solution.py:407
  27.7 0.0 copy-start.3
  27.7 1.0 %copy-done.3 = f32[16,32,512]{2,1,0:T(8,128)} copy-done((f32[16,32,512]{2,1,0:T(8,128)}, f32[16,32,512]{2,1,0:T(8,128)S(1)}, u32[]{:S(2)}) %copy-start.3) | copy-done | bytes 1048600
  28.6 0.0 copy-start.4
  28.6 0.6 %copy-done.4 = f32[32,128]{1,0:T(8,128)} copy-done((f32[32,128]{1,0:T(8,128)}, f32[32,128]{1,0:T(8,128)S(1)}, u32[]{:S(2)}) %copy-start.4) | copy-done | bytes 16408
  29.2 3.9 %expand.1 = f32[16,32,512]{2,1,0:T(8,128)} custom-call(f32[16,32,512]{2,1,0:T(8,128)} %copy-done.3, f32[32,128]{1,0:T(8,128)} %copy-done.4), custom_call_target="tpu_custom_call" | custom-call | tf_op jit(solution)/shard_map/expand/pallas_call | solution.py:435
Async XLA Ops:
  0.0 1.2 %copy-start = (f32[16,32,512]{2,1,0:T(8,128)S(1)}, f32[16,32,512]{2,1,0:T(8,128)}, u32[]{:S(2)}) copy-start(f32[16,32,512]{2,1,0:T(8,128)} %f_hbm.1) | copy-start | bytes 3145732
  1.2 1.2 %copy-start.1 = (f32[16,32,512]{2,1,0:T(8,128)S(1)}, f32[16,32,512]{2,1,0:T(8,128)}, u32[]{:S(2)}) copy-start(f32[16,32,512]{2,1,0:T(8,128)} %b_hbm.1) | copy-start | bytes 3145732
  2.5 1.2 %copy-start.2 = (f32[16,32,512]{2,1,0:T(8,128)S(1)}, f32[16,32,512]{2,1,0:T(8,128)}, u32[]{:S(2)}) copy-start(f32[16,32,512]{2,1,0:T(8,128)} %p_hbm.1) | copy-start | bytes 3145732
  27.7 1.0 %copy-start.3 = (f32[16,32,512]{2,1,0:T(8,128)}, f32[16,32,512]{2,1,0:T(8,128)S(1)}, u32[]{:S(2)}) copy-start(f32[16,32,512]{2,1,0:T(8,128)S(1)} %get-tuple-element.7.fine_ref) | copy-start | bytes 3145732
  28.6 0.6 %copy-start.4 = (f32[32,128]{1,0:T(8,128)}, f32[32,128]{1,0:T(8,128)S(1)}, u32[]{:S(2)}) copy-start(f32[32,128]{1,0:T(8,128)S(1)} %get-tuple-element.8.e_ref) | copy-start | bytes 49156

commit v2 on v1

--- a/solution.py
+++ b/solution.py
@@ -69,8 +69,18 @@
     return (dot(down, hi) + dot(down, lo)) * (1.0 / POOL**3)
 
 
+def expand(flat, rows):
+    lanes = flat.shape[1] * POOL
+    across = members(flat.shape[1], lanes, False)
+    hi, lo = split(flat)
+    wide = dot(hi, across) + dot(lo, across)
+    down = members(rows, flat.shape[0], True)
+    hi, lo = split(wide)
+    return dot(down, hi) + dot(down, lo)
+
+
 def cycle_kernel(
-    nb, ng, f_hbm, b_hbm, p_hbm, fine_hbm, e_ref,
+    nb, ng, f_hbm, b_hbm, p_hbm, fine_hbm, tall_ref,
     V0, B, V1, V2, F, CX, CY, CZ, W, D, T, ysend, yrecv, yface, ygain,
     ACC, GB, GR, KX, KY, KZ, KW, DD,
     lsem, fsend, frecv, csend, crecv,
@@ -364,7 +374,7 @@
         q = q[1:-1] - v + KW[span] * s
         DD[span] = decay * v + gain * q
         e = e + DD[center]
-    e_ref[...] = e.reshape(cx * cy, cz)
+    tall_ref[...] = expand(e.reshape(cx * cy, cz), cx * ny).reshape(cx, 1, ny, nz)
 
     for a in range(4):
         for way in range(4):
@@ -377,19 +387,6 @@
             def _():
                 coarse_copy(a, o).wait_send()
     store.wait()
-
-
-def expand_kernel(fine_ref, e_ref, out_ref):
-    planes, ny, nz = fine_ref.shape
-    cy, cz = e_ref.shape
-    across = members(cz, nz, False)
-    hi, lo = split(e_ref[...])
-    wide = dot(hi, across) + dot(lo, across)
-    down = members(ny, cy, True)
-    hi, lo = split(wide)
-    tall = dot(down, hi) + dot(down, lo)
-    for k in range(planes):
-        out_ref[k] = fine_ref[k] + tall
 
 
 def per_device(nb, ng, right_side, inv_density, pressure):
@@ -403,15 +400,15 @@
     padded = pltpu.VMEM((nx + 2, ny, nz), f32)
     coarse = pltpu.VMEM((ex, ey, cz), f32)
     dma = pltpu.SemaphoreType.DMA
-    hbm = pl.BlockSpec(memory_space=pl.ANY)
-    fine, e = pl.pallas_call(
+    hbm = pl.BlockSpec(memory_space=pltpu.HBM)
+    fine, tall = pl.pallas_call(
         functools.partial(cycle_kernel, nb, ng),
         out_shape=(
             jax.ShapeDtypeStruct((nx, ny, nz), f32),
-            jax.ShapeDtypeStruct((cx * cy, cz), f32),
+            jax.ShapeDtypeStruct((cx, 1, ny, nz), f32),
         ),
         in_specs=[hbm] * 3,
-        out_specs=(hbm, pl.BlockSpec(memory_space=pltpu.VMEM)),
+        out_specs=(pl.BlockSpec(memory_space=pl.ANY), pl.BlockSpec(memory_space=pltpu.VMEM)),
         scratch_shapes=[
             padded, padded, padded, padded,
             block,
@@ -428,21 +425,11 @@
             dma((4,)), dma((4, 4)), dma((4, 4)), dma((2, count)), dma((2, count)),
         ],
         compiler_params=pltpu.CompilerParams(
-            collective_id=0, has_side_effects=True, vmem_limit_bytes=40 * 1024 * 1024
+            collective_id=0, has_side_effects=True, vmem_limit_bytes=63 * 1024 * 1024
         ),
         name="cycle",
     )(right_side, inv_density, pressure)
-    return pl.pallas_call(
-        expand_kernel,
-        grid=(cx,),
-        out_shape=jax.ShapeDtypeStruct((nx, ny, nz), f32),
-        in_specs=[
-            pl.BlockSpec((POOL, ny, nz), lambda g: (g, 0, 0)),
-            pl.BlockSpec((cy, cz), lambda g: (g, 0)),
-        ],
-        out_specs=pl.BlockSpec((POOL, ny, nz), lambda g: (g, 0, 0)),
-        name="expand",
-    )(fine, e)
+    return (fine.reshape(cx, POOL, ny, nz) + tall).reshape(nx, ny, nz)
 
 
 def solution(mesh):

time: 33.5 us -> 27.6 us (0.82)
  local copies, waits for them, and re-layouts: 5.24 us -> 0 us
  Pallas kernels: 27.9 us -> 25 us
  other arithmetic: 0 us -> 2.38 us
    unnamed x10 -> x0, local copies, waits for them, and re-layouts: 5.24 us -> none
    pallas_call x1 -> x0, Pallas kernels: 3.93 us -> none  [per_device(): pl.pallas_call(expand_kernel, grid=(cx,), out_shape=jax.ShapeDtypeStruct(...]
    add x0 -> x1, other arithmetic: none -> 2.38 us  [per_device(): return (fine.reshape(cx, POOL, ny, nz) + tall).reshape(nx, ny, nz)]
    pallas_call x1, Pallas kernels: 24 us -> 25 us  [per_device(): pl.pallas_call(functools.partial(cycle_kernel, nb, ng), out_shape=(jax.Sh...]
where the time goes in v2:
time: 27.6 us; the launch traced here: 27.4 us
  Pallas kernels  25 us (91%)
  other arithmetic  2.38 us (9%)
    pallas_call x1, Pallas kernels, per_device(): pl.pallas_call(functools.partial(cycle_kernel, nb, ng), out_shape=(jax.Sh...  25 us
    add x1, other arithmetic, per_device(): return (fine.reshape(cx, POOL, ny, nz) + tall).reshape(nx, ny, nz)  2.38 us

profile of v2, /device:TPU:5, one launch (start us, length us, event | category | flops | bytes accessed | tf_op | source)
XLA Modules:
  0.0 27.4 jit_solution(12529545393402127033)
XLA Ops:
  0.0 25.0 %cycle.1 = (f32[16,32,512]{2,1,0:T(8,128)}, f32[4,1,32,512]{3,2,1,0:T(8,128)}) custom-call(f32[16,32,512]{2,1,0:T(8,128)} %f_hbm.1, f32[16,32,512]{2,1,0:T(8,128)} %b_hbm.1, f32[16,32,512]{2,1,0:T(8,128)} %p_hbm.1), custom_call_target="tpu_custom_call" | custom-call | tf_op jit(solution)/shard_map/cycle/pallas_call | solution.py:404
  25.0 2.4 %bitcast_add_fusion = f32[16,32,512]{2,1,0:T(8,128)} fusion(f32[16,32,512]{2,1,0:T(8,128)} %get-tuple-element.7, f32[4,32,512]{2,1,0:T(8,128)} %bitcast.3), kind=kLoop, calls=%fused_computation | loop fusion | flops 262144 | bytes 2359296 | tf_op jit(solution)/shard_map/add | solution.py:432

commit v3 on v2

--- a/solution.py
+++ b/solution.py
@@ -80,7 +80,7 @@
 
 
 def cycle_kernel(
-    nb, ng, f_hbm, b_hbm, p_hbm, fine_hbm, tall_ref,
+    nb, ng, f_hbm, b_hbm, p_hbm, out_hbm,
     V0, B, V1, V2, F, CX, CY, CZ, W, D, T, ysend, yrecv, yface, ygain,
     ACC, GB, GR, KX, KY, KZ, KW, DD,
     lsem, fsend, frecv, csend, crecv,
@@ -146,12 +146,20 @@
             def _():
                 fine_copy(a, way).wait_recv()
 
+    def needed(a, dx, dg):
+        reach = (CHEB, CHEB - 1)[a]
+        if dg:
+            reach = reach - (abs(dg) - 1) * cy - 1
+        return min(cx, reach - (abs(dx) - 1) * cx) if dx else cx
+
     def coarse_copy(a, o):
         dx, dg = offsets[o]
         G = (GB, GR)[a]
+        n = needed(a, dx, dg)
+        skip = cx - n if dx > 0 else 0
         return pltpu.make_async_remote_copy(
-            src_ref=G.at[pl.ds(hb * cx, cx), pl.ds(hg * cy, cy)],
-            dst_ref=G.at[pl.ds((hb - dx) * cx, cx), pl.ds((hg - dg) * cy, cy)],
+            src_ref=G.at[pl.ds(hb * cx + skip, n), pl.ds(hg * cy, cy)],
+            dst_ref=G.at[pl.ds((hb - dx) * cx + skip, n), pl.ds((hg - dg) * cy, cy)],
             send_sem=csend.at[a, o], recv_sem=crecv.at[a, o],
             device_id={"box": bx + dx, "group": gx + dg}, device_id_type=MESH,
         )
@@ -186,6 +194,15 @@
                     (cx, cy, cz), jnp.float32
                 )
 
+    for a, G in enumerate((GB, GR)):
+        for dx, dg in offsets:
+            rest = cx - needed(a, dx, dg)
+            if rest:
+                G[
+                    pl.ds((hb + dx) * cx + (cx - rest if dx > 0 else 0), rest),
+                    pl.ds((hg + dg) * cy, cy),
+                ] = jnp.zeros((rest, cy, cz), jnp.float32)
+
     neighbours = 0
     for dx, dg in offsets:
         neighbours = neighbours + there(dx, dg).astype(jnp.int32)
@@ -251,6 +268,25 @@
     GB[center] = pool(ACC[...]).reshape(cx, cy, cz)
     coarse_send(0)
 
+    def inner_sweep(i):
+        k0, k1 = CX[i], CX[i + 1]
+        d = D[i] + (k0 + k1)
+        D[i] = d
+        w = (2.0 / 3.0) * inverse(d)
+        W[i] = w
+        t = T[i] + (k0 * V0[i] + k1 * V0[i + 2])
+        T[i] = t
+        V1[i + 1] = (1.0 / 3.0) * V0[i + 1] + w * t
+
+    def both_ends(step):
+        lax.fori_loop(0, 2, lambda j, c: (step(j * (nx - 1)), c)[1], 0)
+
+    def between(step):
+        lax.fori_loop(1, nx - 1, lambda i, c: (step(i), c)[1], 0)
+
+    bottom, top = pl.ds(0, 8), pl.ds(ny - 8, 8)
+    between(inner_sweep)
+
     receive(1, (0, 1, 2, 3))
     CX[0] = edge_face(B[0], B[1])
     CX[nx] = edge_face(B[nx], B[nx + 1])
@@ -275,15 +311,19 @@
         t = add_rows(t, ygain[0, at, :], ygain[1, at, :])
         V1[i + 1] = (1.0 / 3.0) * V0[i + 1] + w * t
 
-    def both_ends(step):
-        lax.fori_loop(0, 2, lambda j, c: (step(j * (nx - 1)), c)[1], 0)
-
-    def between(step):
-        lax.fori_loop(1, nx - 1, lambda i, c: (step(i), c)[1], 0)
+    def edge_sweep(i):
+        at = pl.ds(i, 1)
+        for side, rows, mask in ((0, bottom, low_row), (1, top, high_row)):
+            d = D[i, rows, :] + jnp.where(mask, yface[side, at, :], 0.0)
+            D[i, rows, :] = d
+            w = (2.0 / 3.0) * inverse(d)
+            W[i, rows, :] = w
+            t = T[i, rows, :] + jnp.where(mask, ygain[side, at, :], 0.0)
+            V1[i + 1, rows, :] = (1.0 / 3.0) * V0[i + 1, rows, :] + w * t
 
     both_ends(first_sweep)
     send(2, (0, 1))
-    between(first_sweep)
+    between(edge_sweep)
     pack(2)
     send(2, (2, 3))
 
@@ -302,8 +342,6 @@
     receive(2, (2, 3))
     gains(2)
 
-    bottom, top = pl.ds(0, 8), pl.ds(ny - 8, 8)
-
     def second_rows(i, c):
         at = pl.ds(i, 1)
         V2[i + 1, bottom, :] += jnp.where(low_row, W[i, bottom, :] * ygain[0, at, :], 0.0)
@@ -314,8 +352,6 @@
     send(3, (0, 1))
     pack(3)
     send(3, (2, 3))
-    store = pltpu.make_async_copy(V2.at[inside], fine_hbm, lsem.at[3])
-    store.start()
 
     ACC[...] = jnp.zeros_like(ACC)
 
@@ -374,7 +410,15 @@
         q = q[1:-1] - v + KW[span] * s
         DD[span] = decay * v + gain * q
         e = e + DD[center]
-    tall_ref[...] = expand(e.reshape(cx * cy, cz), cx * ny).reshape(cx, 1, ny, nz)
+    ACC[...] = expand(e.reshape(cx * cy, cz), cx * ny).reshape(cx, ny, nz)
+    stores = []
+    for g in range(cx):
+        tall = ACC[g]
+        for k in range(POOL * g, POOL * (g + 1)):
+            T[k] = V2[k + 1] + tall
+        planes = pl.ds(POOL * g, POOL)
+        stores.append(pltpu.make_async_copy(T.at[planes], out_hbm.at[planes], lsem.at[3 + g]))
+        stores[-1].start()
 
     for a in range(4):
         for way in range(4):
@@ -386,7 +430,8 @@
             @pl.when(there(dx, dg))
             def _():
                 coarse_copy(a, o).wait_send()
-    store.wait()
+    for store in stores:
+        store.wait()
 
 
 def per_device(nb, ng, right_side, inv_density, pressure):
@@ -401,14 +446,11 @@
     coarse = pltpu.VMEM((ex, ey, cz), f32)
     dma = pltpu.SemaphoreType.DMA
     hbm = pl.BlockSpec(memory_space=pltpu.HBM)
-    fine, tall = pl.pallas_call(
+    return pl.pallas_call(
         functools.partial(cycle_kernel, nb, ng),
-        out_shape=(
-            jax.ShapeDtypeStruct((nx, ny, nz), f32),
-            jax.ShapeDtypeStruct((cx, 1, ny, nz), f32),
-        ),
+        out_shape=jax.ShapeDtypeStruct((nx, ny, nz), f32),
         in_specs=[hbm] * 3,
-        out_specs=(pl.BlockSpec(memory_space=pl.ANY), pl.BlockSpec(memory_space=pltpu.VMEM)),
+        out_specs=pl.BlockSpec(memory_space=pl.ANY),
         scratch_shapes=[
             padded, padded, padded, padded,
             block,
@@ -422,14 +464,13 @@
             coarse, coarse,
             pltpu.VMEM((ex - 1, ey, cz), f32),
             coarse, coarse, coarse, coarse,
-            dma((4,)), dma((4, 4)), dma((4, 4)), dma((2, count)), dma((2, count)),
+            dma((3 + cx,)), dma((4, 4)), dma((4, 4)), dma((2, count)), dma((2, count)),
         ],
         compiler_params=pltpu.CompilerParams(
             collective_id=0, has_side_effects=True, vmem_limit_bytes=63 * 1024 * 1024
         ),
         name="cycle",
     )(right_side, inv_density, pressure)
-    return (fine.reshape(cx, POOL, ny, nz) + tall).reshape(nx, ny, nz)
 
 
 def solution(mesh):

time: 27.6 us -> 26.8 us (0.971)
  other arithmetic: 2.38 us -> 0 us
  local copies, waits for them, and re-layouts: 0 us -> 2.29 us
  Pallas kernels: 25 us -> 24.4 us
    add x1 -> x0, other arithmetic: 2.38 us -> none  [per_device(): return (fine.reshape(cx, POOL, ny, nz) + tall).reshape(nx, ny, nz)]
    unnamed x0 -> x1, local copies, waits for them, and re-layouts: none -> 2.29 us
    pallas_call x1, Pallas kernels: 25 us -> 24.4 us  [per_device(): pl.pallas_call(functools.partial(cycle_kernel, nb, ng), out_shape=jax.Sha...]
where the time goes in v3:
time: 26.8 us; the launch traced here: 26.7 us
  Pallas kernels  24.4 us (91%)
  local copies, waits for them, and re-layouts  2.29 us (9%)
    pallas_call x1, Pallas kernels, per_device(): pl.pallas_call(functools.partial(cycle_kernel, nb, ng), out_shape=jax.Sha...  24.4 us
    unnamed x1, local copies, waits for them, and re-layouts  2.29 us

profile of v3, /device:TPU:5, one launch (start us, length us, event | category | flops | bytes accessed | tf_op | source)
XLA Modules:
  0.0 26.7 jit_solution(8843398213596544480)
XLA Ops:
  0.0 24.4 %cycle.1 = f32[16,32,512]{2,1,0:T(8,128)} custom-call(f32[16,32,512]{2,1,0:T(8,128)} %f_hbm.1, f32[16,32,512]{2,1,0:T(8,128)} %b_hbm.1, f32[16,32,512]{2,1,0:T(8,128)} %p_hbm.1), custom_call_target="tpu_custom_call" | custom-call | tf_op jit(solution)/shard_map/cycle/pallas_call | solution.py:449
  24.4 2.3 %copy.5 = f32[16,32,512]{2,1,0:T(8,128)} copy(f32[16,32,512]{2,1,0:T(8,128)} %cycle.1) | data formatting | bytes 2097152

commit v4 on v3

--- a/solution.py
+++ b/solution.py
@@ -467,7 +467,7 @@
             dma((3 + cx,)), dma((4, 4)), dma((4, 4)), dma((2, count)), dma((2, count)),
         ],
         compiler_params=pltpu.CompilerParams(
-            collective_id=0, has_side_effects=True, vmem_limit_bytes=63 * 1024 * 1024
+            collective_id=0, has_side_effects=True, vmem_limit_bytes=52 * 1024 * 1024
         ),
         name="cycle",
     )(right_side, inv_density, pressure)

time: 26.8 us -> 24.8 us (0.925)
  local copies, waits for them, and re-layouts: 2.29 us -> 0.97 us
  Pallas kernels: 24.4 us -> 23.6 us
    unnamed x1, local copies, waits for them, and re-layouts: 2.29 us -> 0.97 us
    pallas_call x1, Pallas kernels: 24.4 us -> 23.6 us  [per_device(): pl.pallas_call(functools.partial(cycle_kernel, nb, ng), out_shape=jax.Sha...]
where the time goes in v4:
time: 24.8 us; the launch traced here: 24.6 us
  Pallas kernels  23.6 us (95%)
  local copies, waits for them, and re-layouts  0.97 us (4%)
    pallas_call x1, Pallas kernels, per_device(): pl.pallas_call(functools.partial(cycle_kernel, nb, ng), out_shape=jax.Sha...  23.6 us
    unnamed x1, local copies, waits for them, and re-layouts  0.97 us

profile of v4, /device:TPU:5, one launch (start us, length us, event | category | flops | bytes accessed | tf_op | source)
XLA Modules:
  0.0 24.6 jit_solution(295439852036825587)
XLA Ops:
  0.0 23.6 %cycle.1 = f32[16,32,512]{2,1,0:T(8,128)S(1)} custom-call(f32[16,32,512]{2,1,0:T(8,128)} %f_hbm.1, f32[16,32,512]{2,1,0:T(8,128)} %b_hbm.1, f32[16,32,512]{2,1,0:T(8,128)} %p_hbm.1), custom_call_target="tpu_custom_call" | custom-call | tf_op jit(solution)/shard_map/cycle/pallas_call | solution.py:449
  23.6 1.0 %copy.5 = f32[16,32,512]{2,1,0:T(8,128)} copy(f32[16,32,512]{2,1,0:T(8,128)S(1)} %cycle.1) | data formatting | bytes 2097152
